TPU v7x, 128 devices: a whole 4x4x4 slice. The times are simulated.
128 devices in a mesh: grp: 8 (over y, z_lo), tp: 16 (over z_hi, x, core).
Axes of the slice: x: 4, y: 4, z: 4 (z_hi: 2, z_lo: 2; z = z_hi * 2 + z_lo), core: 2. Of those that a mesh axis runs over, the one named last changes fastest.
Arguments:
- hidden_rows: bfloat16 [3, 1024, 16384], P(None, 'grp', 'tp'), may hold values from -6 to 6
- join_weight: bfloat16 [3, 16384, 16384], P(None, 'tp', 'grp'), may hold values from -0.02734375 to 0.02734375
- head_weight: bfloat16 [16384, 16384], P('grp', 'tp'), may hold values from -1.5 to 1.5
- teacher_logits: bfloat16 [1024, 16384], P('grp', 'tp'), may hold values from -18 to 260
Outputs:
- joined_rows: bfloat16 [1024, 16384], P('tp', 'grp')
- token_loss: float32 [1024], P('grp')
All inputs are finite; a program needn't handle non-finite values.
Results may differ from a plain program's by a relative error of at most 0.014.
Values may be sent and summed in bfloat16 or wider, within the bound.
A program may use at most 128 MiB of HBM per device.

v0:
```python
import jax
import jax.numpy as jnp
from jax import lax
from jax.sharding import PartitionSpec as P


def merged_2(x, axis, combine):
    everything = jax.tree.map(lambda part: lax.all_gather(part, axis), x)
    leading = jax.tree.map(lambda part: part[0], everything)

    def hop(k, so_far):
        return combine(so_far, jax.tree.map(lambda part: part[k], everything))

    return lax.fori_loop(1, lax.axis_size(axis), hop, leading)


def combine_stats(earlier, later_one):
    target_max = jnp.maximum(earlier[0], later_one[0])
    target_sum = earlier[1] * jnp.exp(earlier[0] - target_max) + later_one[1] * jnp.exp(
        later_one[0] - target_max
    )
    draft_max = jnp.maximum(earlier[2], later_one[2])
    draft_sum = earlier[3] * jnp.exp(earlier[2] - draft_max) + later_one[3] * jnp.exp(
        later_one[2] - draft_max
    )
    return (target_max, target_sum, draft_max, draft_sum)


def local(hidden_rows, join_weight, head_weight, teacher_logits):
    rows_whole = lax.all_gather(hidden_rows, "grp", axis=1, tiled=True)
    token_count = rows_whole.shape[1]
    share_rows = token_count // lax.axis_size("tp")
    segment = rows_whole
    summed = lax.psum(
        jnp.einsum("ltd,lde->te", segment, join_weight, preferred_element_type=jnp.float32), "tp"
    )
    joined_whole = summed.astype(jnp.bfloat16)
    joined_mine = lax.dynamic_slice_in_dim(
        joined_whole, lax.axis_index("tp") * share_rows, share_rows, 0
    )
    segment = joined_whole
    draft_logits = lax.psum_scatter(
        jnp.dot(segment, head_weight, preferred_element_type=jnp.float32).astype(jnp.bfloat16),
        "grp",
        scatter_dimension=0,
        tiled=True,
    ).astype(jnp.float32)
    target_values = teacher_logits.astype(jnp.float32)
    target_max = jnp.max(target_values, axis=1)
    draft_max = jnp.max(draft_logits, axis=1)
    target_exp = jnp.exp(target_values - target_max[:, None])
    draft_exp = jnp.exp(draft_logits - draft_max[:, None])
    target_sum = jnp.sum(target_exp, axis=1)
    draft_sum = jnp.sum(draft_exp, axis=1)
    merged = merged_2((target_max, target_sum, draft_max, draft_sum), "tp", combine_stats)
    target_norm = merged[0] + jnp.log(merged[1])
    draft_norm = merged[2] + jnp.log(merged[3])
    log_target = target_values - target_norm[:, None]
    log_draft = draft_logits - draft_norm[:, None]
    own_terms = jnp.sum(jnp.exp(log_target) * (log_target - log_draft), axis=1)
    token_loss = lax.psum(own_terms, "tp")
    return (joined_mine, token_loss)


def solution(mesh):
    in_specs = (P(None, "grp", "tp"), P(None, "tp", "grp"), P("grp", "tp"), P("grp", "tp"))
    out_specs = (P("tp", "grp"), P("grp"))
    return jax.shard_map(local, mesh=mesh, in_specs=in_specs, out_specs=out_specs, check_vma=False)
```

profile of v0, /device:TPU:1, one launch (start us, length us, event | category | flops | bytes accessed | tf_op | source)
XLA Modules:
  0.0 415.0 jit_solution(17758363426050423929)
XLA Ops:
  7.2 0.0 all-gather.10.cloned.1.call-start
  7.2 0.7 all-gather.10.cloned.1.call-update
  7.9 0.0 reduce-scatter.2.cloned.1.call-start
  7.9 134.0 %all-gather.10.cloned.1.call-done = bf16[3,1024,1024]{2,1,0:T(8,128)(2,1)} async-done(((bf16[3,128,1024]{2,1,0:T(8,128)(2,1)}), bf16[3,1024,1024]{2,1,0:T(8,128)(2,1)}) %all-gather.10.cloned.1.call-update) | async-done | bytes 6291472 | tf_op jit(solution)/shard_map/all_gather | solution.py:30
  142.0 18.8 %convolution_bitcast_fusion = f32[1024,2048]{1,0:T(8,128)} fusion(bf16[3,1024,1024]{2,1,0:T(8,128)(2,1)} %all-gather.10.cloned.1.call-done, bf16[3,1024,2048]{2,1,0:T(8,128)(2,1)} %param.7), kind=kOutput, calls=%fused_computation.14 | convolution fusion | flops 12884901888 | bytes 27262976 | tf_op jit(solution)/shard_map/ltd,lde->te/dot_general | solution.py:35
  160.7 103.2 %all-reduce.1 = bf16[1024,2048]{1,0:T(8,128)(2,1)} all-reduce(f32[1024,2048]{1,0:T(8,128)} %convolution_bitcast_fusion), channel_id=1, replica_groups=mesh['grp'=8,'tp'=16] {'tp'}, use_global_device_ids=true, to_apply=%region_0.0 | all-reduce | flops 2097152 | bytes 12582912 | tf_op jit(solution)/shard_map/psum | solution.py:34
  263.9 0.0 copy-start
  263.9 9.3 %convolution_convert_fusion = bf16[1024,1024]{1,0:T(8,128)(2,1)} fusion(bf16[1024,2048]{1,0:T(8,128)(2,1)} %all-reduce.1, bf16[2048,1024]{1,0:T(8,128)(2,1)} %param.8), kind=kOutput, calls=%fused_computation.15 | convolution fusion | flops 4296015872 | bytes 10485760 | tf_op jit(solution)/shard_map/dot_general | solution.py:43
  273.2 0.0 reduce-scatter.2.cloned.1.call-update
  273.3 0.0 copy-done
  273.3 0.1 reduce_max.36
  273.4 0.2 fusion.15
  273.6 22.9 %all-gather.5 = f32[16,1,128]{2,1,0:T(1,128)S(1)} all-gather(f32[1,1,128]{2,1,0:T(1,128)S(1)} %bitcast.56), channel_id=3, replica_groups=mesh['grp'=8,'tp'=16] {'tp'}, dimensions={0}, use_global_device_ids=true | all-gather | bytes 8704 | tf_op jit(solution)/shard_map/all_gather | solution.py:8
  296.5 20.9 %all-gather.4 = f32[16,1,128]{2,1,0:T(1,128)S(1)} all-gather(f32[1,1,128]{2,1,0:T(1,128)S(1)} %get-tuple-element.256), channel_id=2, replica_groups=mesh['grp'=8,'tp'=16] {'tp'}, dimensions={0}, use_global_device_ids=true | all-gather | bytes 8704 | tf_op jit(solution)/shard_map/all_gather | solution.py:8
  317.5 1.7 constant_dynamic-slice_fusion.4
  319.1 6.6 %reduce-scatter.2.cloned.1.call-done = bf16[128,1024]{1,0:T(8,128)(2,1)} async-done(((bf16[1024,1024]{1,0:T(8,128)(2,1)}), bf16[128,1024]{1,0:T(8,128)(2,1)}) %reduce-scatter.2.cloned.1.call-update) | async-done | bytes 262160 | tf_op jit(solution)/shard_map/reduce_scatter | solution.py:42
  325.8 1.1 reduce_max.40
  326.8 1.2 fusion.17
  328.0 25.8 %all-gather.7 = f32[16,1,128]{2,1,0:T(1,128)S(1)} all-gather(f32[1,1,128]{2,1,0:T(1,128)S(1)} %bitcast.57), channel_id=5, replica_groups=mesh['grp'=8,'tp'=16] {'tp'}, dimensions={0}, use_global_device_ids=true | all-gather | bytes 8704 | tf_op jit(solution)/shard_map/all_gather | solution.py:8
  353.8 19.1 %all-gather.6 = f32[16,1,128]{2,1,0:T(1,128)S(1)} all-gather(f32[1,1,128]{2,1,0:T(1,128)S(1)} %get-tuple-element.254), channel_id=4, replica_groups=mesh['grp'=8,'tp'=16] {'tp'}, dimensions={0}, use_global_device_ids=true | all-gather | bytes 8704 | tf_op jit(solution)/shard_map/all_gather | solution.py:8
  372.9 0.7 while.21
  373.7 1.3 fusion.13
  374.9 33.2 %psum.15 = f32[128]{0:T(128)} all-reduce(f32[128]{0:T(128)S(1)} %fusion.13), channel_id=1, replica_groups=mesh['grp'=8,'tp'=16] {'tp'}, use_global_device_ids=true, to_apply=%region_9.0 | all-reduce | flops 128 | bytes 1024 | tf_op jit(solution)/shard_map/psum | solution.py:61
  (22 shorter events, 0.5 us)
Async XLA Ops:
  7.2 134.8 %all-gather.10.cloned.1.call-start = ((), (), s32[]{:S(2)}) async-start(), calls=%async_computation.1 | async-start | bytes 7077888 | tf_op jit(solution)/shard_map/all_gather | solution.py:30
  7.9 317.9 %reduce-scatter.2.cloned.1.call-start = ((), (), s32[]{:S(2)}) async-start(), calls=%async_computation.2 | async-start | bytes 2359296 | tf_op jit(solution)/shard_map/reduce_scatter | solution.py:42
  263.9 9.4 %copy-start = (bf16[128,1024]{1,0:T(8,128)(2,1)S(1)}, bf16[128,1024]{1,0:T(8,128)(2,1)}, u32[]{:S(2)}) copy-start(bf16[128,1024]{1,0:T(8,128)(2,1)} %param.9) | copy-start | bytes 786436
Sparse Core Ops, SparseCore 0:
  9.6 132.2 all-gather.9
  273.4 52.3 reduce-scatter.1
where the time goes:
time: 416 us; the launch traced here: 415 us
  blocking collectives  225 us (54%)
  waiting for transfers between devices  141 us (34%)
  matrix products  28.1 us (7%)
  between operations  14.1 us (3%)
  other arithmetic  4.35 us (1%)
    all_gather x1, waiting for transfers between devices, local(): rows_whole = lax.all_gather(hidden_rows, 'grp', axis=1, tiled=True)  134 us
    psum x1, blocking collectives, local(): lax.psum(jnp.einsum('ltd,lde->te', segment, join_weight, preferred_elemen...  103 us
    all_gather x4, blocking collectives, merged_2(): everything = jax.tree.map(lambda part: lax.all_gather(part, axis), x)  88.7 us
    psum x1, blocking collectives, local(): token_loss = lax.psum(own_terms, 'tp')  33.2 us
    dot_general x1, matrix products, local(): jnp.einsum('ltd,lde->te', segment, join_weight, preferred_element_type=jn...  18.8 us
    dot_general x1, matrix products, local(): jnp.dot(segment, head_weight, preferred_element_type=jnp.float32)  9.34 us
  transfers between devices with their start and end apart: 2, of which 2 were waited for; matrix products, arithmetic and copies ran while one was open for 0% of the time, Pallas kernels for 0%

commit v1 on v0

v1 whole, which is shorter than its diff:
```python
import jax
import jax.numpy as jnp
from jax import lax
from jax.experimental import pallas as pl
from jax.experimental.pallas import tpu as pltpu
from jax.sharding import PartitionSpec as P

MESH = pl.DeviceIdType.MESH
F32 = jnp.float32
BF16 = jnp.bfloat16

SLOTS = (
    ((0, 0, 0), (0, 0, 1)),
    ((3, 0, 1), (1, 0, 1)),
    ((0, 1, 0), (0, 1, 1)),
    ((3, 0, 0), (1, 0, 0)),
    ((3, 1, 0), (2, 0, 1)),
    ((3, 1, 1), (1, 1, 0)),
    ((1, 1, 1), (2, 0, 0)),
    ((2, 1, 0), (2, 1, 1)),
)
PLACE = {piece: (s, pos) for s, pair in enumerate(SLOTS) for pos, piece in enumerate(pair)}

NSEM = 160


def kernel(
    hid, wj, wh, tl, out_j, out_l,
    W, H, T, X, ACC, S0, R0, S1, R1, Q, S2, R2, JS, LS, RZ, SA, RYA, RYB, SB, RZB, ET, G,
    loc, snd, rcv,
):
    g = lax.axis_index("grp")
    t = lax.axis_index("tp")
    y, zl = g // 2, g % 2
    zh, x, c = t // 8, (t // 2) % 4, t % 2

    def dev(dy=0, dz=0, dx=0, dh=0, dc=0):
        return (
            lax.rem(y + dy, 4) * 2 + lax.rem(zl + dz, 2),
            lax.rem(zh + dh, 2) * 8 + lax.rem(x + dx, 4) * 2 + lax.rem(c + dc, 2),
        )

    def pid(piece):
        dy, dz, half = piece
        return (lax.rem(y + dy, 4) * 2 + lax.rem(zl + dz, 2)) * 2 + half

    keys = {}
    sent = []

    def remote(key, src, dst, **to):
        k = keys.setdefault(key, len(keys))
        return pltpu.make_async_remote_copy(
            src_ref=src, dst_ref=dst, send_sem=snd.at[k], recv_sem=rcv.at[k],
            device_id=dev(**to), device_id_type=MESH,
        )

    def send(key, src, dst, **to):
        copy = remote(key, src, dst, **to)
        copy.start()
        sent.append(copy)

    def arrived(key, dst, **to):
        remote(key, dst, dst, **to).wait_recv()

    def own_rows(half):
        return pltpu.make_async_copy(
            hid.at[:, pl.ds(half * 64, 64), :], X.at[pid((0, 0, half))], loc.at[half]
        )

    loads = [pltpu.make_async_copy(wj.at[l], W.at[l], loc.at[2 + l]) for l in range(3)]
    load_h = pltpu.make_async_copy(wh, H, loc.at[5])
    load_t = pltpu.make_async_copy(tl, T, loc.at[6])
    own_rows(0).start()
    own_rows(1).start()
    for load in loads:
        load.start()
    load_t.start()
    load_h.start()

    peers = (
        [dict(dy=k) for k in (1, 2, 3)] + [dict(dz=1), dict(dc=1), dict(dh=1)]
        + [dict(dx=k) for k in (1, 2, 3)] + [dict(dx=k, dh=1) for k in (1, 2, 3)]
    )
    barrier = pltpu.get_barrier_semaphore()
    for to in peers:
        pl.semaphore_signal(barrier, inc=1, device_id=dev(**to), device_id_type=MESH)
    pl.semaphore_wait(barrier, len(peers))

    def rows(piece, part=None):
        if part is None:
            return X.at[pid(piece)]
        return X.at[pid(piece), :, pl.ds(part * 32, 32), :]

    def send_own(half, way, **to):
        send(("A", way, half), hid.at[:, pl.ds(half * 64, 64), :], rows((0, 0, half)), **to)

    UP, DOWN = dict(dy=1), dict(dy=3)
    send_own(1, "up", **UP)
    send_own(1, "down", **DOWN)
    send_own(0, "z", dz=1)
    send_own(0, "up", **UP)
    send_own(0, "down", **DOWN)
    send_own(1, "z", dz=1)

    def pass_on(name, piece, part, **to):
        send(("A", name), rows(piece, part), rows(piece, part), **to)

    def got(name, piece, part=None):
        arrived(name, rows(piece, part), dy=1)

    def relay_b():
        got(("A", "down", 1), (1, 0, 1))
        pass_on("sb", (1, 0, 1), None, **DOWN)
        got(("A", "up", 1), (3, 0, 1))
        pass_on("zb'", (3, 0, 1), None, dz=1)
        pass_on("zb''", (1, 0, 1), None, dz=1)

    def relay_c():
        got(("A", "z", 0), (0, 1, 0))
        pass_on("za up", (0, 1, 0), None, **UP)
        pass_on("za down", (0, 1, 0), None, **DOWN)

    def relay_d():
        got(("A", "up", 0), (3, 0, 0))
        pass_on("sa up", (3, 0, 0), 0, **UP)
        got(("A", "down", 0), (1, 0, 0))
        pass_on("sa down", (1, 0, 0), 1, **DOWN)

    def relay_e():
        got(("A", "za up"), (3, 1, 0))
        pass_on("zsa up", (3, 1, 0), 0, **UP)

    def relay_f():
        got(("A", "zb'"), (3, 1, 1))
        pass_on("zsb", (3, 1, 1), None, **UP)

    def relay_g():
        got(("A", "za down"), (1, 1, 0))
        pass_on("zsa down", (1, 1, 0), 1, **DOWN)

    def wait_rows(s):
        if s == 0:
            own_rows(0).wait()
            own_rows(1).wait()
            for load in loads:
                load.wait()
        if s == 2:
            got(("A", "z", 1), (0, 1, 1))
        if s == 4:
            got(("A", "sb"), (2, 0, 1))
        if s == 6:
            got(("A", "zb''"), (1, 1, 1))
            got(("A", "sa up"), (2, 0, 0), 0)
            got(("A", "sa down"), (2, 0, 0), 1)
        if s == 7:
            got(("A", "zsa up"), (2, 1, 0), 0)
            got(("A", "zsa down"), (2, 1, 0), 1)
            got(("A", "zsb"), (2, 1, 1))

    def st0(s):
        wait_rows(s)
        p0, p1 = pid(SLOTS[s][0]), pid(SLOTS[s][1])

        def joined(col):
            total = None
            for l in range(3):
                a = jnp.concatenate([X[p0, l], X[p1, l]], axis=0)
                part = jnp.dot(a, W[l, :, pl.ds(pl.multiple_of(col, 512), 512)], preferred_element_type=F32)
                total = part if total is None else total + part
            return total

        def theirs(k, carry):
            S0[s, :, pl.ds(pl.multiple_of(k * 512, 512), 512)] = joined((1 - c) * 1024 + k * 512).astype(BF16)
            return carry

        def mine(k, carry):
            ACC[s, :, pl.ds(pl.multiple_of(k * 512, 512), 512)] = joined(c * 1024 + k * 512)
            return carry

        lax.fori_loop(0, 2, theirs, 0)
        send(("B0", s), S0.at[s], R0.at[s], dc=1)
        lax.fori_loop(0, 2, mine, 0)

    def st1(s):
        arrived(("B0", s), R0.at[s], dc=1)
        for j in (2, 1, 3, 0):
            cols = pl.ds(pl.multiple_of(lax.rem(x + j, 4) * 256, 256), 256)
            v = ACC[s, :, cols] + R0[s, :, cols].astype(F32)
            if j:
                S1[s, j - 1] = v.astype(BF16)
                send(("B1", s, j), S1.at[s, j - 1], R1.at[s, j - 1], dx=j)
            else:
                Q[s] = v

    def st2(s):
        v = Q[s]
        for j in (1, 3, 2):
            arrived(("B1", s, j), R1.at[s, j - 1], dx=j)
            v = v + R1[s, j - 1].astype(F32)
        S2[s] = v.astype(BF16)
        send(("B2", s), S2.at[s], R2.at[s], dh=1)

    def st3(s):
        arrived(("B2", s), R2.at[s], dh=1)
        JS[s, c, x] = (S2[s].astype(F32) + R2[s].astype(F32)).astype(BF16)
        for j in (2, 1, 3):
            send(("C1", s, j), JS.at[s, c, x], JS.at[s, c, x], dx=j)

    def st4(s):
        for j in (1, 3, 2):
            arrived(("C1", s, j), JS.at[s, c, lax.rem(x + 4 - j, 4)], dx=j)
        send(("C0", s), JS.at[s, c], JS.at[s, c], dc=1)

    def st5(s):
        if s == 0:
            load_h.wait()
        arrived(("C0", s), JS.at[s, 1 - c], dc=1)

        def head(k, carry):
            cols = pl.ds(pl.multiple_of(k * 256, 256), 256)
            a = jnp.concatenate([JS[s, i, j] for i in range(2) for j in range(4)], axis=1)
            LS[s, :, cols] = jnp.dot(a, H[:, cols], preferred_element_type=F32).astype(BF16)
            return carry

        lax.fori_loop(0, 4, head, 0)

    def logits(piece):
        s, pos = PLACE[piece]
        return LS.at[s, pl.ds(pos * 64, 64), :]

    def value(piece):
        s, pos = PLACE[piece]
        return LS[s, pos * 64 : pos * 64 + 64, :].astype(F32)

    def st6(s):
        for piece in SLOTS[s]:
            dy, dz, half = piece
            if half == 0 and dz == 1:
                send(("DZ", dy), logits(piece), RZ.at[dy], dz=1)
            if half == 1 and dy != 0:
                send(("DYB", dz, dy), logits(piece), RYB.at[dz, dy - 1], dy=dy)

    def over_z(dy):
        arrived(("DZ", dy), RZ.at[dy], dz=1)
        SA[dy - 1] = (value((dy, 0, 0)) + RZ[dy].astype(F32)).astype(BF16)
        send(("DYA", dy), SA.at[dy - 1], RYA.at[dy - 1], dy=dy)

    def over_y():
        v = value((0, 1, 1))
        for dy in (1, 3, 2):
            arrived(("DYB", 1, dy), RYB.at[1, dy - 1], dy=dy)
            v = v + RYB[1, dy - 1].astype(F32)
        SB[...] = v.astype(BF16)
        send(("DZB",), SB, RZB, dz=1)

    def teacher_stats():
        load_t.wait()
        v = T[...].astype(F32)
        top = jnp.max(v, axis=1, keepdims=True)
        e = jnp.exp(v - top)
        ET[...] = e
        return top, jnp.sum(e, axis=1, keepdims=True)

    def finish(target_max, target_sum):
        va = value((0, 0, 0))
        arrived(("DZ", 0), RZ.at[0], dz=1)
        va = va + RZ[0].astype(F32)
        for dy in (1, 3, 2):
            arrived(("DYA", dy), RYA.at[dy - 1], dy=dy)
            va = va + RYA[dy - 1].astype(F32)
        vb = value((0, 0, 1))
        for dy in (1, 3, 2):
            arrived(("DYB", 0, dy), RYB.at[0, dy - 1], dy=dy)
            vb = vb + RYB[0, dy - 1].astype(F32)
        arrived(("DZB",), RZB, dz=1)
        vb = vb + RZB[...].astype(F32)
        draft = jnp.concatenate([va, vb], axis=0)
        draft_max = jnp.max(draft, axis=1, keepdims=True)
        shifted = draft - draft_max
        draft_sum = jnp.sum(jnp.exp(shifted), axis=1, keepdims=True)
        cross = jnp.sum(ET[...] * ((T[...].astype(F32) - target_max) - shifted), axis=1, keepdims=True)
        lane = lax.broadcasted_iota(jnp.int32, (128, 128), 1)
        table = jnp.zeros((128, 128), F32)
        for k, column in enumerate((target_max, target_sum, draft_max, draft_sum, cross)):
            table = jnp.where(lane == k, column, table)
        G[t] = jnp.transpose(table)[0:8, :]
        send(("E0",), G.at[t], G.at[t], dc=1)
        pair = pl.ds((t // 2) * 2, 2)
        arrived(("E0",), G.at[t], dc=1)
        for k, to in enumerate([dict(dx=j, dh=1) for j in (2, 1, 3)] + [dict(dh=1)] + [dict(dx=j) for j in (2, 1, 3)]):
            send(("E1", k), G.at[pair], G.at[pair], **to)
        for k in (4, 5, 6, 0, 1, 2, 3):
            arrived(("E1", k), G.at[pair], dh=1)
        tm, ts, dm, ds, cr = (G[:, k, :] for k in range(5))
        tm_all = jnp.max(tm, axis=0, keepdims=True)
        dm_all = jnp.max(dm, axis=0, keepdims=True)
        tw = jnp.exp(tm - tm_all)
        ts_all = jnp.sum(ts * tw, axis=0, keepdims=True)
        ds_all = jnp.sum(ds * jnp.exp(dm - dm_all), axis=0, keepdims=True)
        cr_all = jnp.sum(tw * (cr + ((tm - tm_all) - (dm - dm_all)) * ts), axis=0, keepdims=True)
        out_l[...] = cr_all / ts_all - jnp.log(ts_all) + jnp.log(ds_all)

    def joined_out():
        place = 0
        for s in range(8):
            for pos in range(2):
                place = place + jnp.where(pid(SLOTS[s][pos]) == t, s * 2 + pos, 0)
        for i in range(2):
            for j in range(4):
                col = (i * 4 + j) * 256
                out_j[:, col : col + 256] = JS[place // 2, i, j, pl.ds(pl.multiple_of((place % 2) * 64, 64), 64), :]

    st0(0)
    st1(0)
    tmax, tsum = teacher_stats()
    relay_b()
    relay_c()
    st0(1)
    st2(0)
    st1(1)
    st3(0)
    st2(1)
    st4(0)
    st3(1)
    st5(0)
    relay_d()
    st0(2)
    st4(1)
    st1(2)
    st0(3)
    st5(1)
    st1(3)
    st2(2)
    st2(3)
    relay_e()
    st0(4)
    st3(2)
    st1(4)
    st3(3)
    relay_f()
    st4(2)
    st2(4)
    st4(3)
    st5(2)
    st5(3)
    st3(4)
    relay_g()
    st0(5)
    st4(4)
    for s in (2, 1, 3):
        st6(s)
    st1(5)
    st5(4)
    st6(4)
    st2(5)
    over_z(3)
    st0(6)
    st0(7)
    st1(6)
    st3(5)
    st1(7)
    st4(5)
    st5(5)
    st6(5)
    st2(6)
    over_z(1)
    st2(7)
    st3(6)
    st3(7)
    st4(6)
    st4(7)
    st5(6)
    st6(6)
    st5(7)
    st6(7)
    over_z(2)
    over_y()
    joined_out()
    finish(tmax, tsum)
    for copy in sent:
        copy.wait_send()
    assert len(keys) <= NSEM, len(keys)


def local(hidden_rows, join_weight, head_weight, teacher_logits):
    vmem = pltpu.VMEM
    joined, loss = pl.pallas_call(
        kernel,
        out_shape=(jax.ShapeDtypeStruct((64, 2048), BF16), jax.ShapeDtypeStruct((1, 128), F32)),
        in_specs=[pl.BlockSpec(memory_space=pl.ANY)] * 4,
        out_specs=[pl.BlockSpec(memory_space=pltpu.VMEM)] * 2,
        scratch_shapes=[
            vmem((3, 1024, 2048), BF16),
            vmem((2048, 1024), BF16),
            vmem((128, 1024), BF16),
            vmem((16, 3, 64, 1024), BF16),
            vmem((8, 128, 1024), F32),
            vmem((8, 128, 1024), BF16),
            vmem((8, 128, 1024), BF16),
            vmem((8, 3, 128, 256), BF16),
            vmem((8, 3, 128, 256), BF16),
            vmem((8, 128, 256), F32),
            vmem((8, 128, 256), BF16),
            vmem((8, 128, 256), BF16),
            vmem((8, 2, 4, 128, 256), BF16),
            vmem((8, 128, 1024), BF16),
            vmem((4, 64, 1024), BF16),
            vmem((3, 64, 1024), BF16),
            vmem((3, 64, 1024), BF16),
            vmem((2, 3, 64, 1024), BF16),
            vmem((64, 1024), BF16),
            vmem((64, 1024), BF16),
            vmem((128, 1024), F32),
            vmem((16, 8, 128), F32),
            pltpu.SemaphoreType.DMA((7,)),
            pltpu.SemaphoreType.DMA((NSEM,)),
            pltpu.SemaphoreType.DMA((NSEM,)),
        ],
        compiler_params=pltpu.CompilerParams(
            collective_id=0, has_side_effects=True, vmem_limit_bytes=60 * 1024 * 1024
        ),
        cost_estimate=pl.CostEstimate(flops=17179869184, bytes_accessed=18350080, transcendentals=262144),
    )(hidden_rows, join_weight, head_weight, teacher_logits)
    return joined, loss.reshape(128)


def solution(mesh):
    in_specs = (P(None, "grp", "tp"), P(None, "tp", "grp"), P("grp", "tp"), P("grp", "tp"))
    out_specs = (P("tp", "grp"), P("grp"))
    return jax.shard_map(local, mesh=mesh, in_specs=in_specs, out_specs=out_specs, check_vma=False)
```

time: 416 us -> 150 us (0.36)
  blocking collectives: 225 us -> 0 us
  Pallas kernels: 0 us -> 147 us
  waiting for transfers between devices: 141 us -> 0 us
  matrix products: 28.1 us -> 0 us
  between operations: 14.1 us -> 0.64 us
  other arithmetic: 4.35 us -> 0 us
    pallas_call x0 -> x1, Pallas kernels: none -> 147 us  [local(): pl.pallas_call(kernel, out_shape=(jax.ShapeDtypeStruct((64, 2048), BF16),...]
    psum x2 -> x0, blocking collectives: 136 us -> none  [the longest x1 103 us: local(): lax.psum(jnp.einsum('ltd,lde->te', segment, join_weight, preferred_elemen...]
    all_gather x1 -> x0, waiting for transfers between devices: 134 us -> none  [local(): rows_whole = lax.all_gather(hidden_rows, 'grp', axis=1, tiled=True)]
    all_gather x4 -> x0, blocking collectives: 88.7 us -> none  [merged_2(): everything = jax.tree.map(lambda part: lax.all_gather(part, axis), x)]
    dot_general x2 -> x0, matrix products: 28.1 us -> none  [the longest x1 18.8 us: local(): jnp.einsum('ltd,lde->te', segment, join_weight, preferred_element_type=jn...]
    reduce_scatter x1 -> x0, waiting for transfers between devices: 6.63 us -> none  [local(): lax.psum_scatter(jnp.dot(segment, head_weight, preferred_element_type=jnp...]
  transfers between devices with their start and end apart: 2 -> 0, of which waited for: 2 -> 0; matrix products, arithmetic and copies ran while one was open for 0% -> 0% of each run, Pallas kernels for 0% -> 0%
where the time goes in v1:
time: 150 us
  Pallas kernels  147 us (98%)
  local copies, waits for them, and re-layouts  2.8 us (2%)
    pallas_call x1, Pallas kernels, local(): pl.pallas_call(kernel, out_shape=(jax.ShapeDtypeStruct((64, 2048), BF16),...  147 us

profile of v1, /device:TPU:1, one launch (start us, length us, event | category | flops | bytes accessed | tf_op | source)
XLA Modules:
  0.0 149.9 jit_solution(6578712170331150469)
XLA Ops:
  0.6 146.5 %shard_map.59 = (bf16[64,2048]{1,0:T(8,128)(2,1)}, f32[1,128]{1,0:T(1,128)}) custom-call(bf16[3,128,1024]{2,1,0:T(8,128)(2,1)} %hid.1, bf16[3,1024,2048]{2,1,0:T(8,128)(2,1)} %wj.1, bf16[2048,1024]{1,0:T(8,128)(2,1)} %wh.1, bf16[128,1024]{1,0:T(8,128)(2,1)} %tl.1), custom_call_target="tpu_custom_call" | custom-call | flops 17179869184 | bytes 18350080 | tf_op jit(solution)/shard_map/pallas_call | solution.py:387
  147.1 1.7 %copy.8 = bf16[64,2048]{1,0:T(8,128)(2,1)} copy(bf16[64,2048]{1,0:T(8,128)(2,1)} %get-tuple-element.8) | data formatting | bytes 524288
  148.8 1.1 copy.9

commit v2 on v1

v2 whole, which is shorter than its diff:
```python
import jax
import jax.numpy as jnp
from jax import lax
from jax.experimental import pallas as pl
from jax.experimental.pallas import tpu as pltpu
from jax.sharding import PartitionSpec as P

MESH = pl.DeviceIdType.MESH
F32 = jnp.float32
BF16 = jnp.bfloat16

SLOTS = (
    ((0, 0, 0), (0, 0, 1)),
    ((3, 0, 1), (1, 0, 1)),
    ((0, 1, 0), (3, 0, 0)),
    ((1, 1, 0), (3, 1, 1)),
    ((2, 0, 0), (2, 0, 1)),
    ((1, 1, 1), (2, 1, 1)),
    ((2, 1, 0), (1, 0, 0)),
    ((0, 1, 1), (3, 1, 0)),
)
WIDE = (7,)
DIRECT = (
    (3, 1, 0),
    (3, 0, 0),
    (1, 0, 0),
    (1, 1, 0),
    (2, 1, 0),
    (2, 0, 0),
)
PLACE = {piece: (s, pos) for s, slot in enumerate(SLOTS) for pos, piece in enumerate(slot)}

START = (
    ("up", (0, 0, 1), None),
    ("down", (0, 0, 1), None),
    ("z", (0, 0, 0), None),
    ("up", (0, 0, 0), None),
    ("down", (0, 0, 0), 0),
    ("z", (0, 0, 1), 0),
)
LATER = {
    "up": (("up", (0, 1, 0), 0), ("up", (3, 0, 0), None), ("up", (3, 1, 1), None), ("up", (0, 1, 0), 1)),
    "down": (("down", (0, 1, 0), None), ("down", (1, 0, 1), None), ("down", (1, 1, 0), None), ("down", (0, 0, 0), 1)),
    "z": (("z", (3, 0, 1), 0), ("z", (3, 0, 1), 1), ("z", (1, 0, 1), 0), ("z", (1, 0, 1), 1), ("z", (0, 0, 1), 1)),
}
TO = {"up": dict(dy=1), "down": dict(dy=3), "z": dict(dz=1)}


def lands(copy):
    way, (dy, dz, half), _ = copy
    return (dy + {"up": 3, "down": 1, "z": 0}[way]) % 4, dz ^ (way == "z"), half


COPIES = START + sum(LATER.values(), ())
CROSS = ((2, 1), (1, 1), (3, 1), (0, 1), (2, 0), (1, 0), (3, 0))
NSEM = 96
POOL = 40


def kernel(
    hid, wj, wh, tl, out_j, out_l,
    W, H, T, X, ACC, S0, R0, S1, R1, Q, S2, R2, JS, S8, R8, J8, LS, RZ, SA, RYA, RYB, SB, RZB, RD,
    ET, TAB, G, loc, snd, rcv,
):
    g = lax.axis_index("grp")
    t = lax.axis_index("tp")
    y, zl = g // 2, g % 2
    zh, x, c = t // 8, (t // 2) % 4, t % 2

    def dev(dy=0, dz=0, dx=0, dh=0, dc=0):
        return (
            lax.rem(y + dy, 4) * 2 + lax.rem(zl + dz, 2),
            lax.rem(zh + dh, 2) * 8 + lax.rem(x + dx, 4) * 2 + lax.rem(c + dc, 2),
        )

    def pid(piece):
        dy, dz, half = piece
        return (lax.rem(y + dy, 4) * 2 + lax.rem(zl + dz, 2)) * 2 + half

    keys = {}
    sent = []

    def remote(key, src, dst, turn, **to):
        k = keys.setdefault(key, len(keys))
        return pltpu.make_async_remote_copy(
            src_ref=src, dst_ref=dst, send_sem=snd.at[turn], recv_sem=rcv.at[k],
            device_id=dev(**to), device_id_type=MESH,
        )

    def send(key, src, dst, **to):
        if len(sent) >= POOL:
            sent[-POOL].wait_send()
        copy = remote(key, src, dst, len(sent) % POOL, **to)
        copy.start()
        sent.append(copy)

    def arrived(key, dst, **to):
        remote(key, dst, dst, 0, **to).wait_recv()

    def own_rows(half):
        return pltpu.make_async_copy(
            hid.at[:, pl.ds(half * 64, 64), :], X.at[pid((0, 0, half))], loc.at[half]
        )

    loads = [pltpu.make_async_copy(wj.at[l], W.at[l], loc.at[2 + l]) for l in range(3)]
    load_h = pltpu.make_async_copy(wh, H, loc.at[5])
    load_t = pltpu.make_async_copy(tl, T, loc.at[6])

    peers = (
        [dict(dy=k) for k in (1, 2, 3)] + [dict(dz=1), dict(dc=1)]
        + [dict(dx=k, dh=h) for k, h in CROSS] + [dict(dy=k, dz=1) for k in (1, 2, 3)]
    )
    barrier = pltpu.get_barrier_semaphore()
    for to in peers:
        pl.semaphore_signal(barrier, inc=1, device_id=dev(**to), device_id_type=MESH)
    own_rows(0).start()
    own_rows(1).start()
    for load in loads:
        load.start()
    load_t.start()
    load_h.start()
    pl.semaphore_wait(barrier, len(peers))

    def rows(piece, part=None):
        if part is None:
            return X.at[pid(piece)]
        return X.at[pid(piece), :, pl.ds(part * 32, 32), :]

    waited = set()

    def need(piece, part=None):
        for copy in COPIES:
            if lands(copy) == piece and copy not in waited and (part is None or copy[2] in (None, part)):
                waited.add(copy)
                arrived(copy, rows(piece, copy[2]), **TO[copy[0]])

    def move(copy):
        way, piece, part = copy
        if piece[:2] == (0, 0):
            first, count = (piece[2] * 64, 64) if part is None else (piece[2] * 64 + part * 32, 32)
            src = hid.at[:, pl.ds(first, count), :]
        else:
            need(piece, part)
            src = rows(piece, part)
        send(copy, src, rows(piece, part), **TO[way])

    def onward(way, k):
        move(LATER[way][k])

    for copy in START:
        move(copy)

    def size(s):
        return 64 * len(SLOTS[s])

    def top(s):
        return pl.ds(0, size(s))

    def st0(s):
        for piece in SLOTS[s]:
            need(piece)
        if s == 0:
            own_rows(0).wait()
            own_rows(1).wait()
            for load in loads:
                load.wait()
        places = [pid(piece) for piece in SLOTS[s]]

        def joined(col):
            total = None
            for l in range(3):
                a = jnp.concatenate([X[p, l] for p in places], axis=0)
                part = jnp.dot(a, W[l, :, pl.ds(pl.multiple_of(col, 512), 512)], preferred_element_type=F32)
                total = part if total is None else total + part
            return total

        def theirs(k, carry):
            S0[s, top(s), pl.ds(pl.multiple_of(k * 512, 512), 512)] = joined((1 - c) * 1024 + k * 512).astype(BF16)
            return carry

        def mine(k, carry):
            ACC[s, top(s), pl.ds(pl.multiple_of(k * 512, 512), 512)] = joined(c * 1024 + k * 512)
            return carry

        lax.fori_loop(0, 2, theirs, 0)
        send(("B0", s), S0.at[s, top(s)], R0.at[s, top(s)], dc=1)
        lax.fori_loop(0, 2, mine, 0)

    def pair_sum(s, first, count):
        cols = pl.ds(pl.multiple_of(first, count), count)
        return ACC[s, top(s), cols] + R0[s, top(s), cols].astype(F32)

    def st1(s):
        arrived(("B0", s), R0.at[s, top(s)], dc=1)
        if s in WIDE:
            w = WIDE.index(s)
            for j, (dx, dh) in enumerate(CROSS):
                S8[w, j, top(s)] = pair_sum(s, (lax.rem(zh + dh, 2) * 4 + lax.rem(x + dx, 4)) * 128, 128).astype(BF16)
                send(("B1", s), S8.at[w, j, top(s)], R8.at[w, j, top(s)], dx=dx, dh=dh)
            Q[s, top(s), 0:128] = pair_sum(s, (zh * 4 + x) * 128, 128)
            return
        for j in (2, 1, 3):
            S1[s, j - 1, top(s)] = pair_sum(s, lax.rem(x + j, 4) * 256, 256).astype(BF16)
            send(("B1", s), S1.at[s, j - 1, top(s)], R1.at[s, j - 1, top(s)], dx=j)
        Q[s, top(s)] = pair_sum(s, x * 256, 256)

    def st2(s):
        if s in WIDE:
            w = WIDE.index(s)
            v = Q[s, top(s), 0:128]
            arrived(("B1", s), R8.at[w, :, top(s)], dx=1)
            for j in range(7):
                v = v + R8[w, j, top(s)].astype(F32)
            mine = J8.at[w, c, zh * 4 + x, top(s)]
            mine[...] = v.astype(BF16)
            for j, (dx, dh) in enumerate(CROSS):
                send(("C1", s), mine, mine, dx=dx, dh=dh)
            return
        v = Q[s, top(s)]
        arrived(("B1", s), R1.at[s, :, top(s)], dx=1)
        for j in (1, 2, 3):
            v = v + R1[s, j - 1, top(s)].astype(F32)
        S2[s, top(s)] = v.astype(BF16)
        send(("B2", s), S2.at[s, top(s)], R2.at[s, top(s)], dh=1)

    def st3(s):
        arrived(("B2", s), R2.at[s, top(s)], dh=1)
        mine = JS.at[s, c, x, top(s)]
        mine[...] = (S2[s, top(s)].astype(F32) + R2[s, top(s)].astype(F32)).astype(BF16)
        for j in (2, 1, 3):
            send(("C1", s), mine, mine, dx=j)

    def blocks(s):
        if s in WIDE:
            return J8, WIDE.index(s), 8
        return JS, s, 4

    def st4(s):
        buf, k, parts = blocks(s)
        arrived(("C1", s), buf.at[k, c, pl.ds(0, parts - 1), top(s)], dx=1)
        send(("C0", s), buf.at[k, c, :, top(s)], buf.at[k, c, :, top(s)], dc=1)

    def st5(s):
        if s == 0:
            load_h.wait()
        buf, k, parts = blocks(s)
        arrived(("C0", s), buf.at[k, 1 - c, :, top(s)], dc=1)
        cuts = [(i, j) for i in range(2) for j in range(parts)]

        def head(n, carry):
            cols = pl.ds(pl.multiple_of(n * 256, 256), 256)
            a = jnp.concatenate([buf[k, i, j, top(s)] for i, j in cuts], axis=1)
            LS[s, top(s), cols] = jnp.dot(a, H[:, cols], preferred_element_type=F32).astype(BF16)
            return carry

        lax.fori_loop(0, 4, head, 0)

    def logits(piece):
        s, pos = PLACE[piece]
        return LS.at[s, pl.ds(pos * 64, 64), :]

    def value(piece):
        s, pos = PLACE[piece]
        return LS[s, pos * 64 : pos * 64 + 64, :].astype(F32)

    def st6(s):
        for piece in SLOTS[s]:
            dy, dz, half = piece
            if piece in DIRECT:
                send(("DD", piece), logits(piece), RD.at[DIRECT.index(piece)], dy=dy, dz=dz)
            elif half == 0 and dz == 1:
                send(("DZ", dy), logits(piece), RZ.at[dy], dz=1)
            elif half == 1 and dy != 0:
                send(("DYB", dz, dy), logits(piece), RYB.at[dz, dy - 1], dy=dy)
        for pos, piece in enumerate(SLOTS[s]):
            buf, k, parts = blocks(s)

            @pl.when(pid(piece) == t)
            def _():
                width = 1024 // parts
                for i in range(2):
                    for j in range(parts):
                        col = i * 1024 + j * width
                        out_j[:, col : col + width] = buf[k, i, j, pos * 64 : pos * 64 + 64, :]

    def over_z(dy):
        arrived(("DZ", dy), RZ.at[dy], dz=1)
        SA[dy - 1] = (value((dy, 0, 0)) + RZ[dy].astype(F32)).astype(BF16)
        send(("DYA", dy), SA.at[dy - 1], RYA.at[dy - 1], dy=dy)

    def over_y():
        v = value((0, 1, 1))
        for dy in (1, 3, 2):
            if (dy, 1, 1) not in DIRECT:
                arrived(("DYB", 1, dy), RYB.at[1, dy - 1], dy=dy)
                v = v + RYB[1, dy - 1].astype(F32)
        SB[...] = v.astype(BF16)
        send(("DZB",), SB, RZB, dz=1)

    lane = lax.broadcasted_iota(jnp.int32, (64, 128), 1)

    def teacher():
        load_t.wait()
        for half in range(2):
            mine = pl.ds(half * 64, 64)
            v = T[mine, :].astype(F32)
            peak = jnp.max(v, axis=1, keepdims=True)
            e = jnp.exp(v - peak)
            ET[mine, :] = e
            TAB[mine, :] = jnp.where(lane == 0, peak, jnp.sum(e, axis=1, keepdims=True))

    def fin_half(half):
        v = value((0, 0, half))
        parts = []
        if half == 0:
            parts.append((("DZ", 0), RZ.at[0]))
            parts += [(("DYA", dy), RYA.at[dy - 1]) for dy in (1, 3, 2) if (dy, 0, 0) not in DIRECT]
        else:
            parts += [(("DYB", 0, dy), RYB.at[0, dy - 1]) for dy in (1, 3, 2) if (dy, 0, 1) not in DIRECT]
            parts.append((("DZB",), RZB))
        parts += [(("DD", piece), RD.at[k]) for k, piece in enumerate(DIRECT) if piece[2] == half]
        for key, buf in parts:
            arrived(key, buf, dy=1)
            v = v + buf[...].astype(F32)
        mine = pl.ds(half * 64, 64)
        draft_max = jnp.max(v, axis=1, keepdims=True)
        shifted = v - draft_max
        draft_sum = jnp.sum(jnp.exp(shifted), axis=1, keepdims=True)
        table = TAB[mine, :]
        cross = jnp.sum(ET[mine, :] * ((T[mine, :].astype(F32) - table[:, 0:1]) - shifted), axis=1, keepdims=True)
        for k, column in ((2, draft_max), (3, draft_sum), (4, cross)):
            table = jnp.where(lane == k, column, table)
        TAB[mine, :] = table

    def fin0():
        G[t] = jnp.transpose(TAB[...])[0:8, :]
        send(("E0",), G.at[t], G.at[t], dc=1)

    pair = pl.ds((t // 2) * 2, 2)

    def fin1():
        arrived(("E0",), G.at[t], dc=1)
        for j, (dx, dh) in enumerate(CROSS):
            send(("E1",), G.at[pair], G.at[pair], dx=dx, dh=dh)

    def fin2():
        arrived(("E1",), G.at[pl.ds(0, 14)], dx=1)
        tm, ts, dm, ds, cr = (G[:, k, :] for k in range(5))
        tm_all = jnp.max(tm, axis=0, keepdims=True)
        dm_all = jnp.max(dm, axis=0, keepdims=True)
        tw = jnp.exp(tm - tm_all)
        ts_all = jnp.sum(ts * tw, axis=0, keepdims=True)
        ds_all = jnp.sum(ds * jnp.exp(dm - dm_all), axis=0, keepdims=True)
        cr_all = jnp.sum(tw * (cr + ((tm - tm_all) - (dm - dm_all)) * ts), axis=0, keepdims=True)
        out_l[...] = cr_all / ts_all - jnp.log(ts_all) + jnp.log(ds_all)

    teacher()
    st0(0)
    st1(0)
    onward("z", 0)
    onward("down", 0)
    st0(1)
    onward("up", 0)
    st2(0)
    st1(1)
    onward("z", 1)
    onward("down", 1)
    onward("up", 1)
    st0(2)
    onward("z", 2)
    st3(0)
    st2(1)
    st1(2)
    st0(3)
    onward("down", 2)
    onward("up", 2)
    onward("z", 3)
    st4(0)
    st1(3)
    st5(0)
    st2(2)
    st3(1)
    st0(4)
    onward("up", 3)
    st2(3)
    onward("down", 3)
    st6(0)
    st1(4)
    st3(2)
    onward("z", 4)
    st4(1)
    st5(1)
    st6(1)
    st3(3)
    st0(5)
    st2(4)
    st4(2)
    st1(5)
    st0(6)
    st5(2)
    st3(4)
    st6(2)
    st0(7)
    st2(5)
    st4(3)
    st1(6)
    st1(7)
    st5(3)
    st6(3)
    st4(4)
    st5(4)
    st3(5)
    st6(4)
    st2(6)
    st2(7)
    st4(5)
    st3(6)
    st5(5)
    st6(5)
    st4(7)
    st5(7)
    st6(7)
    st4(6)
    st5(6)
    st6(6)
    over_y()
    fin_half(0)
    fin_half(1)
    fin0()
    fin1()
    fin2()
    for copy in sent[-POOL:]:
        copy.wait_send()
    assert len(keys) <= NSEM, len(keys)


def hand_over(joined, loss, out_j, out_l):
    out_j[...] = joined[...]
    out_l[...] = loss[0]


def local(hidden_rows, join_weight, head_weight, teacher_logits):
    vmem = pltpu.VMEM
    n, w, d = len(SLOTS), max(1, len(WIDE)), max(1, len(DIRECT))
    joined, loss = pl.pallas_call(
        kernel,
        out_shape=(jax.ShapeDtypeStruct((64, 2048), BF16), jax.ShapeDtypeStruct((1, 128), F32)),
        in_specs=[pl.BlockSpec(memory_space=pl.ANY)] * 4,
        out_specs=[pl.BlockSpec(memory_space=pltpu.VMEM)] * 2,
        scratch_shapes=[
            vmem((3, 1024, 2048), BF16),
            vmem((2048, 1024), BF16),
            vmem((128, 1024), BF16),
            vmem((16, 3, 64, 1024), BF16),
            vmem((n, 128, 1024), F32),
            vmem((n, 128, 1024), BF16),
            vmem((n, 128, 1024), BF16),
            vmem((n, 3, 128, 256), BF16),
            vmem((n, 3, 128, 256), BF16),
            vmem((n, 128, 256), F32),
            vmem((n, 128, 256), BF16),
            vmem((n, 128, 256), BF16),
            vmem((n, 2, 4, 128, 256), BF16),
            vmem((w, 7, 128, 128), BF16),
            vmem((w, 7, 128, 128), BF16),
            vmem((w, 2, 8, 128, 128), BF16),
            vmem((n, 128, 1024), BF16),
            vmem((4, 64, 1024), BF16),
            vmem((3, 64, 1024), BF16),
            vmem((3, 64, 1024), BF16),
            vmem((2, 3, 64, 1024), BF16),
            vmem((64, 1024), BF16),
            vmem((64, 1024), BF16),
            vmem((d, 64, 1024), BF16),
            vmem((128, 1024), F32),
            vmem((128, 128), F32),
            vmem((16, 8, 128), F32),
            pltpu.SemaphoreType.DMA((7,)),
            pltpu.SemaphoreType.DMA((POOL,)),
            pltpu.SemaphoreType.DMA((NSEM,)),
        ],
        compiler_params=pltpu.CompilerParams(
            collective_id=0, has_side_effects=True, vmem_limit_bytes=60 * 1024 * 1024
        ),
        cost_estimate=pl.CostEstimate(flops=17179869184, bytes_accessed=18350080, transcendentals=262144),
    )(hidden_rows, join_weight, head_weight, teacher_logits)
    return pl.pallas_call(
        hand_over,
        out_shape=(jax.ShapeDtypeStruct((64, 2048), BF16), jax.ShapeDtypeStruct((128,), F32)),
        in_specs=[pl.BlockSpec(memory_space=pltpu.VMEM)] * 2,
        out_specs=[pl.BlockSpec(memory_space=pltpu.VMEM)] * 2,
    )(joined, loss)


def solution(mesh):
    in_specs = (P(None, "grp", "tp"), P(None, "tp", "grp"), P("grp", "tp"), P("grp", "tp"))
    out_specs = (P("tp", "grp"), P("grp"))
    return jax.shard_map(local, mesh=mesh, in_specs=in_specs, out_specs=out_specs, check_vma=False)
```

time: 150 us -> 99.3 us (0.66)
  Pallas kernels: 147 us -> 98.5 us
  local copies, waits for them, and re-layouts: 2.8 us -> 0 us
    pallas_call x1, Pallas kernels: 147 us -> 96.9 us  [local(): pl.pallas_call(kernel, out_shape=(jax.ShapeDtypeStruct((64, 2048), BF16),...]
    unnamed x2 -> x0, local copies, waits for them, and re-layouts: 2.8 us -> none
    pallas_call x0 -> x1, Pallas kernels: none -> 1.68 us  [local(): pl.pallas_call(hand_over, out_shape=(jax.ShapeDtypeStruct((64, 2048), BF1...]
where the time goes in v2:
time: 99.3 us; the launch traced here: 99.2 us
  Pallas kernels  98.5 us (99%)
    pallas_call x1, Pallas kernels, local(): pl.pallas_call(kernel, out_shape=(jax.ShapeDtypeStruct((64, 2048), BF16),...  96.9 us

profile of v2, /device:TPU:1, one launch (start us, length us, event | category | flops | bytes accessed | tf_op | source)
XLA Modules:
  0.0 99.2 jit_solution(7850795338741346519)
XLA Ops:
  0.6 96.9 %shard_map.59 = (bf16[64,2048]{1,0:T(8,128)(2,1)}, f32[1,128]{1,0:T(1,128)}) custom-call(bf16[3,128,1024]{2,1,0:T(8,128)(2,1)} %hid.1, bf16[3,1024,2048]{2,1,0:T(8,128)(2,1)} %wj.1, bf16[2048,1024]{1,0:T(8,128)(2,1)} %wh.1, bf16[128,1024]{1,0:T(8,128)(2,1)} %tl.1), custom_call_target="tpu_custom_call" | custom-call | flops 17179869184 | bytes 18350080 | tf_op jit(solution)/shard_map/pallas_call | solution.py:445
  97.5 1.7 %shard_map.60 = (bf16[64,2048]{1,0:T(8,128)(2,1)}, f32[128]{0:T(128)}) custom-call(bf16[64,2048]{1,0:T(8,128)(2,1)} %get-tuple-element.4.joined, f32[1,128]{1,0:T(1,128)} %get-tuple-element.5.loss), custom_call_target="tpu_custom_call" | custom-call | tf_op jit(solution)/shard_map/pallas_call | solution.py:487

commit v3 on v2

--- a/solution.py
+++ b/solution.py
@@ -15,33 +15,30 @@
     ((0, 1, 0), (3, 0, 0)),
     ((1, 1, 0), (3, 1, 1)),
     ((2, 0, 0), (2, 0, 1)),
-    ((1, 1, 1), (2, 1, 1)),
-    ((2, 1, 0), (1, 0, 0)),
-    ((0, 1, 1), (3, 1, 0)),
+    ((1, 1, 1), (3, 1, 0)),
+    ((2, 1, 0), (0, 1, 1)),
+    ((2, 1, 1), (1, 0, 0)),
 )
 WIDE = (7,)
 DIRECT = (
-    (3, 1, 0),
-    (3, 0, 0),
-    (1, 0, 0),
-    (1, 1, 0),
     (2, 1, 0),
     (2, 0, 0),
+    (2, 1, 1),
 )
 PLACE = {piece: (s, pos) for s, slot in enumerate(SLOTS) for pos, piece in enumerate(slot)}
 
 START = (
-    ("up", (0, 0, 1), None),
-    ("down", (0, 0, 1), None),
-    ("z", (0, 0, 0), None),
-    ("up", (0, 0, 0), None),
-    ("down", (0, 0, 0), 0),
-    ("z", (0, 0, 1), 0),
+    ("up", (0, 0, 1), (0, 64)),
+    ("down", (0, 0, 1), (0, 64)),
+    ("z", (0, 0, 0), (0, 64)),
+    ("up", (0, 0, 0), (0, 64)),
+    ("down", (0, 0, 0), (0, 32)),
+    ("z", (0, 0, 1), (0, 16)),
 )
 LATER = {
-    "up": (("up", (0, 1, 0), 0), ("up", (3, 0, 0), None), ("up", (3, 1, 1), None), ("up", (0, 1, 0), 1)),
-    "down": (("down", (0, 1, 0), None), ("down", (1, 0, 1), None), ("down", (1, 1, 0), None), ("down", (0, 0, 0), 1)),
-    "z": (("z", (3, 0, 1), 0), ("z", (3, 0, 1), 1), ("z", (1, 0, 1), 0), ("z", (1, 0, 1), 1), ("z", (0, 0, 1), 1)),
+    "up": (("up", (0, 1, 0), (0, 32)), ("up", (3, 0, 0), (0, 64)), ("up", (0, 1, 0), (32, 32)), ("up", (3, 1, 1), (0, 64))),
+    "down": (("down", (0, 1, 0), (0, 64)), ("down", (1, 0, 1), (0, 64)), ("down", (1, 1, 0), (0, 64)), ("down", (0, 0, 0), (32, 32))),
+    "z": (("z", (3, 0, 1), (0, 16)), ("z", (3, 0, 1), (16, 16)), ("z", (3, 0, 1), (32, 16)), ("z", (3, 0, 1), (48, 16)), ("z", (1, 0, 1), (0, 16)), ("z", (1, 0, 1), (16, 16)), ("z", (1, 0, 1), (32, 16)), ("z", (1, 0, 1), (48, 16)), ("z", (0, 0, 1), (16, 16)), ("z", (0, 0, 1), (32, 16)), ("z", (0, 0, 1), (48, 16))),
 }
 TO = {"up": dict(dy=1), "down": dict(dy=3), "z": dict(dz=1)}
 
@@ -53,8 +50,8 @@
 
 COPIES = START + sum(LATER.values(), ())
 CROSS = ((2, 1), (1, 1), (3, 1), (0, 1), (2, 0), (1, 0), (3, 0))
-NSEM = 96
-POOL = 40
+NSEM = 104
+POOL = 48
 
 
 def kernel(
@@ -108,7 +105,7 @@
 
     peers = (
         [dict(dy=k) for k in (1, 2, 3)] + [dict(dz=1), dict(dc=1)]
-        + [dict(dx=k, dh=h) for k, h in CROSS] + [dict(dy=k, dz=1) for k in (1, 2, 3)]
+        + [dict(dx=k, dh=h, dc=i) for k, h in CROSS for i in range(2)] + [dict(dy=k, dz=1) for k in (2,)]
     )
     barrier = pltpu.get_barrier_semaphore()
     for to in peers:
@@ -121,24 +118,23 @@
     load_h.start()
     pl.semaphore_wait(barrier, len(peers))
 
-    def rows(piece, part=None):
-        if part is None:
-            return X.at[pid(piece)]
-        return X.at[pid(piece), :, pl.ds(part * 32, 32), :]
+    def rows(piece, part):
+        return X.at[pid(piece), :, pl.ds(*part), :]
 
     waited = set()
 
-    def need(piece, part=None):
+    def need(piece, part=(0, 64)):
         for copy in COPIES:
-            if lands(copy) == piece and copy not in waited and (part is None or copy[2] in (None, part)):
+            first, count = copy[2]
+            meets = first < part[0] + part[1] and part[0] < first + count
+            if lands(copy) == piece and meets and copy not in waited:
                 waited.add(copy)
                 arrived(copy, rows(piece, copy[2]), **TO[copy[0]])
 
     def move(copy):
         way, piece, part = copy
         if piece[:2] == (0, 0):
-            first, count = (piece[2] * 64, 64) if part is None else (piece[2] * 64 + part * 32, 32)
-            src = hid.at[:, pl.ds(first, count), :]
+            src = hid.at[:, pl.ds(piece[2] * 64 + part[0], part[1]), :]
         else:
             need(piece, part)
             src = rows(piece, part)
@@ -155,6 +151,16 @@
 
     def top(s):
         return pl.ds(0, size(s))
+
+    def joined(s, core):
+        places = [pid(piece) for piece in SLOTS[s]]
+        cols = pl.ds(pl.multiple_of(core * 1024, 1024), 1024)
+        total = None
+        for l in range(3):
+            a = jnp.concatenate([X[p, l] for p in places], axis=0)
+            part = jnp.dot(a, W[l, :, cols], preferred_element_type=F32)
+            total = part if total is None else total + part
+        return total
 
     def st0(s):
         for piece in SLOTS[s]:
@@ -164,27 +170,11 @@
             own_rows(1).wait()
             for load in loads:
                 load.wait()
-        places = [pid(piece) for piece in SLOTS[s]]
-
-        def joined(col):
-            total = None
-            for l in range(3):
-                a = jnp.concatenate([X[p, l] for p in places], axis=0)
-                part = jnp.dot(a, W[l, :, pl.ds(pl.multiple_of(col, 512), 512)], preferred_element_type=F32)
-                total = part if total is None else total + part
-            return total
-
-        def theirs(k, carry):
-            S0[s, top(s), pl.ds(pl.multiple_of(k * 512, 512), 512)] = joined((1 - c) * 1024 + k * 512).astype(BF16)
-            return carry
-
-        def mine(k, carry):
-            ACC[s, top(s), pl.ds(pl.multiple_of(k * 512, 512), 512)] = joined(c * 1024 + k * 512)
-            return carry
-
-        lax.fori_loop(0, 2, theirs, 0)
+        S0[s, top(s)] = joined(s, 1 - c).astype(BF16)
         send(("B0", s), S0.at[s, top(s)], R0.at[s, top(s)], dc=1)
-        lax.fori_loop(0, 2, mine, 0)
+
+    def st9(s):
+        ACC[s, top(s)] = joined(s, c)
 
     def pair_sum(s, first, count):
         cols = pl.ds(pl.multiple_of(first, count), count)
@@ -247,13 +237,8 @@
         arrived(("C0", s), buf.at[k, 1 - c, :, top(s)], dc=1)
         cuts = [(i, j) for i in range(2) for j in range(parts)]
 
-        def head(n, carry):
-            cols = pl.ds(pl.multiple_of(n * 256, 256), 256)
-            a = jnp.concatenate([buf[k, i, j, top(s)] for i, j in cuts], axis=1)
-            LS[s, top(s), cols] = jnp.dot(a, H[:, cols], preferred_element_type=F32).astype(BF16)
-            return carry
-
-        lax.fori_loop(0, 4, head, 0)
+        a = jnp.concatenate([buf[k, i, j, top(s)] for i, j in cuts], axis=1)
+        LS[s, top(s)] = jnp.dot(a, H[...], preferred_element_type=F32).astype(BF16)
 
     def logits(piece):
         s, pos = PLACE[piece]
@@ -334,17 +319,13 @@
 
     def fin0():
         G[t] = jnp.transpose(TAB[...])[0:8, :]
-        send(("E0",), G.at[t], G.at[t], dc=1)
-
-    pair = pl.ds((t // 2) * 2, 2)
-
-    def fin1():
-        arrived(("E0",), G.at[t], dc=1)
-        for j, (dx, dh) in enumerate(CROSS):
-            send(("E1",), G.at[pair], G.at[pair], dx=dx, dh=dh)
+        for dx, dh in CROSS:
+            for dc in (1, 0):
+                send(("E",), G.at[t], G.at[t], dx=dx, dh=dh, dc=dc)
+        send(("E",), G.at[t], G.at[t], dc=1)
 
     def fin2():
-        arrived(("E1",), G.at[pl.ds(0, 14)], dx=1)
+        arrived(("E",), G.at[pl.ds(0, 15)], dc=1)
         tm, ts, dm, ds, cr = (G[:, k, :] for k in range(5))
         tm_all = jnp.max(tm, axis=0, keepdims=True)
         dm_all = jnp.max(dm, axis=0, keepdims=True)
@@ -354,80 +335,95 @@
         cr_all = jnp.sum(tw * (cr + ((tm - tm_all) - (dm - dm_all)) * ts), axis=0, keepdims=True)
         out_l[...] = cr_all / ts_all - jnp.log(ts_all) + jnp.log(ds_all)
 
+    st0(0)
+    st9(0)
     teacher()
-    st0(0)
     st1(0)
-    onward("z", 0)
+    st2(0)
     onward("down", 0)
     st0(1)
+    onward("z", 0)
+    onward("z", 1)
+    st9(1)
+    st1(1)
+    st3(0)
     onward("up", 0)
-    st2(0)
-    st1(1)
-    onward("z", 1)
+    onward("z", 2)
+    onward("z", 3)
     onward("down", 1)
+    st2(1)
     onward("up", 1)
     st0(2)
-    onward("z", 2)
-    st3(0)
-    st2(1)
+    st9(2)
+    st4(0)
     st1(2)
+    onward("z", 4)
+    onward("z", 5)
+    st5(0)
     st0(3)
+    st9(3)
+    onward("z", 6)
+    st3(1)
+    st1(3)
+    st2(2)
     onward("down", 2)
     onward("up", 2)
-    onward("z", 3)
-    st4(0)
-    st1(3)
-    st5(0)
-    st2(2)
-    st3(1)
-    st0(4)
+    onward("z", 7)
+    onward("z", 8)
     onward("up", 3)
-    st2(3)
-    onward("down", 3)
-    st6(0)
-    st1(4)
-    st3(2)
-    onward("z", 4)
     st4(1)
     st5(1)
-    st6(1)
-    st3(3)
+    st3(2)
+    onward("z", 9)
+    st0(4)
+    st2(3)
+    st9(4)
+    st1(4)
+    onward("z", 10)
+    onward("down", 3)
     st0(5)
-    st2(4)
+    st9(5)
     st4(2)
     st1(5)
+    st6(1)
+    st6(0)
+    st5(2)
+    st3(3)
+    st2(4)
+    st6(2)
     st0(6)
-    st5(2)
+    st9(6)
+    st2(5)
+    st1(6)
+    st0(7)
     st3(4)
-    st6(2)
-    st0(7)
-    st2(5)
+    st9(7)
+    st1(7)
     st4(3)
-    st1(6)
-    st1(7)
     st5(3)
+    st2(6)
     st6(3)
+    st3(5)
     st4(4)
     st5(4)
-    st3(5)
     st6(4)
-    st2(6)
+    st3(6)
     st2(7)
     st4(5)
-    st3(6)
     st5(5)
     st6(5)
+    st4(6)
+    st5(6)
+    st6(6)
     st4(7)
     st5(7)
     st6(7)
-    st4(6)
-    st5(6)
-    st6(6)
+    over_z(1)
+    over_z(3)
     over_y()
+    fin_half(1)
     fin_half(0)
-    fin_half(1)
     fin0()
-    fin1()
     fin2()
     for copy in sent[-POOL:]:
         copy.wait_send()

time: 99.3 us -> 94.7 us (0.954)
  Pallas kernels: 98.5 us -> 93.9 us
    pallas_call x1, Pallas kernels: 96.9 us -> 92.2 us  [local(): pl.pallas_call(kernel, out_shape=(jax.ShapeDtypeStruct((64, 2048), BF16),...]
where the time goes in v3:
time: 94.7 us; the launch traced here: 94.6 us
  Pallas kernels  93.9 us (99%)
    pallas_call x1, Pallas kernels, local(): pl.pallas_call(kernel, out_shape=(jax.ShapeDtypeStruct((64, 2048), BF16),...  92.2 us

profile of v3, /device:TPU:1, one launch (start us, length us, event | category | flops | bytes accessed | tf_op | source)
XLA Modules:
  0.0 94.6 jit_solution(17034377092460920015)
XLA Ops:
  0.6 92.2 %shard_map.59 = (bf16[64,2048]{1,0:T(8,128)(2,1)}, f32[1,128]{1,0:T(1,128)}) custom-call(bf16[3,128,1024]{2,1,0:T(8,128)(2,1)} %hid.1, bf16[3,1024,2048]{2,1,0:T(8,128)(2,1)} %wj.1, bf16[2048,1024]{1,0:T(8,128)(2,1)} %wh.1, bf16[128,1024]{1,0:T(8,128)(2,1)} %tl.1), custom_call_target="tpu_custom_call" | custom-call | flops 17179869184 | bytes 18350080 | tf_op jit(solution)/shard_map/pallas_call | solution.py:441
  92.9 1.7 %shard_map.60 = (bf16[64,2048]{1,0:T(8,128)(2,1)}, f32[128]{0:T(128)}) custom-call(bf16[64,2048]{1,0:T(8,128)(2,1)} %get-tuple-element.4.joined, f32[1,128]{1,0:T(1,128)} %get-tuple-element.5.loss), custom_call_target="tpu_custom_call" | custom-call | tf_op jit(solution)/shard_map/pallas_call | solution.py:483

commit v4 on v3

--- a/solution.py
+++ b/solution.py
@@ -50,14 +50,14 @@
 
 COPIES = START + sum(LATER.values(), ())
 CROSS = ((2, 1), (1, 1), (3, 1), (0, 1), (2, 0), (1, 0), (3, 0))
-NSEM = 104
-POOL = 48
+NSEM = 80
+POOL = 40
 
 
 def kernel(
     hid, wj, wh, tl, out_j, out_l,
     W, H, T, X, ACC, S0, R0, S1, R1, Q, S2, R2, JS, S8, R8, J8, LS, RZ, SA, RYA, RYB, SB, RZB, RD,
-    ET, TAB, G, loc, snd, rcv,
+    ET, TAB, G, J, loc, snd, rcv,
 ):
     g = lax.axis_index("grp")
     t = lax.axis_index("tp")
@@ -104,8 +104,7 @@
     load_t = pltpu.make_async_copy(tl, T, loc.at[6])
 
     peers = (
-        [dict(dy=k) for k in (1, 2, 3)] + [dict(dz=1), dict(dc=1)]
-        + [dict(dx=k, dh=h, dc=i) for k, h in CROSS for i in range(2)] + [dict(dy=k, dz=1) for k in (2,)]
+        [dict(dy=1), dict(dy=3), dict(dz=1), dict(dc=1), dict(dh=1)] + [dict(dx=k) for k in (1, 2, 3)]
     )
     barrier = pltpu.get_barrier_semaphore()
     for to in peers:
@@ -266,7 +265,7 @@
                 for i in range(2):
                     for j in range(parts):
                         col = i * 1024 + j * width
-                        out_j[:, col : col + width] = buf[k, i, j, pos * 64 : pos * 64 + 64, :]
+                        J[:, col : col + width] = buf[k, i, j, pos * 64 : pos * 64 + 64, :]
 
     def over_z(dy):
         arrived(("DZ", dy), RZ.at[dy], dz=1)
@@ -281,6 +280,8 @@
                 v = v + RYB[1, dy - 1].astype(F32)
         SB[...] = v.astype(BF16)
         send(("DZB",), SB, RZB, dz=1)
+
+    hand_j = pltpu.make_async_copy(J, out_j, loc.at[0])
 
     lane = lax.broadcasted_iota(jnp.int32, (64, 128), 1)
 
@@ -341,25 +342,25 @@
     st1(0)
     st2(0)
     onward("down", 0)
+    onward("z", 0)
     st0(1)
-    onward("z", 0)
+    st9(1)
     onward("z", 1)
-    st9(1)
+    onward("z", 2)
     st1(1)
+    onward("up", 0)
     st3(0)
-    onward("up", 0)
-    onward("z", 2)
     onward("z", 3)
-    onward("down", 1)
     st2(1)
     onward("up", 1)
     st0(2)
     st9(2)
+    onward("z", 4)
     st4(0)
     st1(2)
-    onward("z", 4)
+    onward("down", 1)
+    st5(0)
     onward("z", 5)
-    st5(0)
     st0(3)
     st9(3)
     onward("z", 6)
@@ -367,24 +368,24 @@
     st1(3)
     st2(2)
     onward("down", 2)
+    onward("z", 7)
     onward("up", 2)
-    onward("z", 7)
     onward("z", 8)
-    onward("up", 3)
     st4(1)
+    onward("z", 9)
     st5(1)
     st3(2)
-    onward("z", 9)
     st0(4)
     st2(3)
+    onward("up", 3)
     st9(4)
     st1(4)
     onward("z", 10)
-    onward("down", 3)
     st0(5)
     st9(5)
     st4(2)
     st1(5)
+    onward("down", 3)
     st6(1)
     st6(0)
     st5(2)
@@ -395,15 +396,15 @@
     st9(6)
     st2(5)
     st1(6)
+    st3(4)
     st0(7)
-    st3(4)
     st9(7)
+    st4(3)
     st1(7)
-    st4(3)
     st5(3)
+    st3(5)
     st2(6)
     st6(3)
-    st3(5)
     st4(4)
     st5(4)
     st6(4)
@@ -418,13 +419,15 @@
     st4(7)
     st5(7)
     st6(7)
-    over_z(1)
+    hand_j.start()
     over_z(3)
     over_y()
+    over_z(1)
     fin_half(1)
     fin_half(0)
     fin0()
     fin2()
+    hand_j.wait()
     for copy in sent[-POOL:]:
         copy.wait_send()
     assert len(keys) <= NSEM, len(keys)
@@ -442,7 +445,7 @@
         kernel,
         out_shape=(jax.ShapeDtypeStruct((64, 2048), BF16), jax.ShapeDtypeStruct((1, 128), F32)),
         in_specs=[pl.BlockSpec(memory_space=pl.ANY)] * 4,
-        out_specs=[pl.BlockSpec(memory_space=pltpu.VMEM)] * 2,
+        out_specs=[pl.BlockSpec(memory_space=pl.ANY), pl.BlockSpec(memory_space=pltpu.VMEM)],
         scratch_shapes=[
             vmem((3, 1024, 2048), BF16),
             vmem((2048, 1024), BF16),
@@ -471,6 +474,7 @@
             vmem((128, 1024), F32),
             vmem((128, 128), F32),
             vmem((16, 8, 128), F32),
+            vmem((64, 2048), BF16),
             pltpu.SemaphoreType.DMA((7,)),
             pltpu.SemaphoreType.DMA((POOL,)),
             pltpu.SemaphoreType.DMA((NSEM,)),

time: 94.7 us -> 93.3 us (0.985)
  Pallas kernels: 93.9 us -> 92.6 us
    pallas_call x1, Pallas kernels: 92.2 us -> 90.9 us  [local(): pl.pallas_call(kernel, out_shape=(jax.ShapeDtypeStruct((64, 2048), BF16),...]
where the time goes in v4:
time: 93.3 us; the launch traced here: 93.2 us
  Pallas kernels  92.6 us (99%)
    pallas_call x1, Pallas kernels, local(): pl.pallas_call(kernel, out_shape=(jax.ShapeDtypeStruct((64, 2048), BF16),...  90.9 us

profile of v4, /device:TPU:1, one launch (start us, length us, event | category | flops | bytes accessed | tf_op | source)
XLA Modules:
  0.0 93.2 jit_solution(13228313538209477459)
XLA Ops:
  0.6 90.9 %shard_map.59 = (bf16[64,2048]{1,0:T(8,128)(2,1)}, f32[1,128]{1,0:T(1,128)}) custom-call(bf16[3,128,1024]{2,1,0:T(8,128)(2,1)} %hid.1, bf16[3,1024,2048]{2,1,0:T(8,128)(2,1)} %wj.1, bf16[2048,1024]{1,0:T(8,128)(2,1)} %wh.1, bf16[128,1024]{1,0:T(8,128)(2,1)} %tl.1), custom_call_target="tpu_custom_call" | custom-call | flops 17179869184 | bytes 18350080 | tf_op jit(solution)/shard_map/pallas_call | solution.py:444
  91.5 1.7 %shard_map.60 = (bf16[64,2048]{1,0:T(8,128)(2,1)}, f32[128]{0:T(128)}) custom-call(bf16[64,2048]{1,0:T(8,128)(2,1)} %get-tuple-element.4.joined, f32[1,128]{1,0:T(1,128)} %get-tuple-element.5.loss), custom_call_target="tpu_custom_call" | custom-call | tf_op jit(solution)/shard_map/pallas_call | solution.py:487
